TPU v7x, 512 devices: a whole 4x8x8 slice. The times are simulated.
512 devices in a mesh: rad: 8 (over y), ang: 64 (over x, z, core).
Axes of the slice: x: 4, y: 8, z: 8, core: 2. Of those that a mesh axis runs over, the one named last changes fastest.
Arguments:
- state: bfloat16 [6, 2, 1024, 256, 128], P(None, None, ('rad', 'ang')), may hold values from -6 to 6
- legendre: bfloat16 [1024, 192, 256], P(('rad', 'ang')), may hold values from -0.375 to 0.375
- radial_ops: bfloat16 [2, 128, 256], replicated, may hold values from -0.375 to 0.375
- base_flow: bfloat16 [3, 384, 128, 1024], P(None, 'ang', 'rad'), may hold values from -6 to 6
- base_field: bfloat16 [3, 384, 128, 1024], P(None, 'ang', 'rad'), may hold values from -6 to 6
- assign: int32 [512, 2], replicated, may hold values from -1 to 511, as said below
- counts: int32 [512], replicated, may hold values from 0 to 2, as said below
Outputs:
- tangent: bfloat16 [6, 2, 1024, 256, 128], P(None, None, ('rad', 'ang'))
Inputs may be any that keep to these rules, and one draw needn't show every extreme that they name: Slot j of device d (d = the rad index times the ang axis's size plus the ang index) holds order assign[d, j] when j < counts[d] and -1 otherwise; each order 0 to 511 is held by exactly one live slot. counts[d] plus the count of the device with the same rad index whose ang index differs by half the ang axis equals 2.
All inputs are finite; a program needn't handle non-finite values.
Results may differ from a plain program's by a relative error of at most 0.01.
Values may be sent and summed in bfloat16 or wider, within the bound.
A program may use at most 128 MiB of HBM per device.

v0:
```python
import math

import jax
import jax.numpy as jnp
from jax import lax
from jax.sharding import PartitionSpec as P

coriolis = 3.0


def cross_product(first_vec, second_vec):
    return jnp.stack(
        [
            first_vec[1] * second_vec[2] - first_vec[2] * second_vec[1],
            first_vec[2] * second_vec[0] - first_vec[0] * second_vec[2],
            first_vec[0] * second_vec[1] - first_vec[1] * second_vec[0],
        ]
    )


def trig_table(orders, points, factor):
    positions = jnp.arange(points, dtype=jnp.int32)
    wrapped = orders[:, None] * positions[None, :] % points
    angles = wrapped.astype(jnp.float32) * (2.0 * math.pi / points)
    stacked = jnp.stack([jnp.cos(angles), -jnp.sin(angles)]) * factor[None, :, None]
    return stacked.astype(jnp.bfloat16)


def colatitude(row_index, lat_rows):
    northern = ((row_index // 2).astype(jnp.float32) + 0.5) * (math.pi / lat_rows)
    return jnp.where(row_index % 2 == 1, math.pi - northern, northern)


def slot_orders(assign, counts):
    capacity = assign.shape[1]
    is_live = jnp.arange(capacity, dtype=jnp.int32)[None, :] < counts[:, None]
    return (jnp.where(is_live, assign, 0), is_live)


def per_device(state, legendre, radial_ops, base_flow, base_field, assign, counts):
    rad_count = lax.axis_size("rad")
    ang_count = lax.axis_size("ang")
    devices = rad_count * ang_count
    capacity = state.shape[2]
    mean_slots = capacity // 2
    degrees = state.shape[3]
    shells = state.shape[4]
    band_rows = base_flow.shape[1]
    shell_rows = base_flow.shape[2]
    lon_points = base_flow.shape[3]
    lat_rows = band_rows * ang_count
    half_lat = legendre.shape[1]
    orders_total = devices * mean_slots
    device = lax.axis_index("rad") * ang_count + lax.axis_index("ang")
    current = state
    orders, is_live = slot_orders(assign, counts)
    slots_here = current.shape[2]
    piece_len = rad_count * slots_here * band_rows * shell_rows
    local_orders = lax.dynamic_index_in_dim(orders, device, 0, keepdims=False)
    local_live = lax.dynamic_index_in_dim(is_live, device, 0, keepdims=False)
    degree_idx = jnp.arange(degrees, dtype=jnp.int32)
    usable = local_live[:, None] & (local_orders[:, None] + degree_idx[None, :] < orders_total)
    masked_rows = legendre * usable[:, None, :].astype(jnp.bfloat16)
    degree_sum = (local_orders[:, None] + degree_idx[None, :]).astype(jnp.float32)
    damping = jnp.where(
        usable, 1.0 / (1.0 + degree_sum * (degree_sum + 1.0) / (degrees * degrees)), 0.0
    )
    grouped = orders.reshape(rad_count, ang_count, slots_here)
    lat_major = jnp.transpose(grouped, (1, 0, 2)).reshape(-1)
    synth_table = trig_table(
        lat_major, lon_points, jnp.full(lat_major.shape, 1.0 / math.sqrt(orders_total), jnp.float32)
    )
    synth_table = synth_table.reshape(2, ang_count, rad_count, slots_here, lon_points)
    anal_factor = jnp.where(lat_major == 0, 1.0, 2.0).astype(jnp.float32) * (
        math.sqrt(orders_total) / lon_points
    )
    anal_table = trig_table(lat_major, lon_points, anal_factor)
    anal_table = anal_table.reshape(2, ang_count, rad_count, slots_here, lon_points)
    row_index = lax.axis_index("ang") * band_rows + jnp.arange(band_rows, dtype=jnp.int32)
    colat_rows = colatitude(row_index, lat_rows)
    axis_dir = jnp.stack([jnp.cos(colat_rows), -jnp.sin(colat_rows), jnp.zeros_like(colat_rows)])[
        :, :, None, None
    ]
    weight = (math.pi / 2 * jnp.sin(colat_rows))[None, :, None, None]
    base_vel = base_flow.astype(jnp.float32)
    magnet = base_field.astype(jnp.float32)
    spin_axis = base_vel + coriolis * axis_dir
    even_part = jnp.einsum(
        "cxsnr,stn->cxstr",
        current[:, :, :, 0::2],
        masked_rows[:, :, 0::2],
        preferred_element_type=jnp.float32,
    )
    odd_part = jnp.einsum(
        "cxsnr,stn->cxstr",
        current[:, :, :, 1::2],
        masked_rows[:, :, 1::2],
        preferred_element_type=jnp.float32,
    )
    grid_vals = jnp.stack([even_part + odd_part, even_part - odd_part], axis=4)
    grid_vals = grid_vals.reshape(
        6, 2, slots_here, ang_count, band_rows, rad_count, shell_rows
    ).astype(jnp.bfloat16)
    grid_vals = jnp.transpose(grid_vals, (0, 1, 3, 5, 2, 4, 6)).reshape(6, 2, ang_count, piece_len)
    spread = lax.all_to_all(
        lax.all_to_all(grid_vals, "rad", split_axis=3, concat_axis=3, tiled=True),
        "ang",
        split_axis=2,
        concat_axis=2,
        tiled=True,
    )
    spread = spread.reshape(6, 2, ang_count, rad_count, slots_here, band_rows, shell_rows)
    fields = jnp.einsum(
        "cxabsqr,xabsk->cqrk", spread, synth_table, preferred_element_type=jnp.float32
    )
    momentum = cross_product(fields[:3], spin_axis) + cross_product(magnet, fields[3:])
    induction = cross_product(fields[:3], magnet) + cross_product(base_vel, fields[3:])
    products = (jnp.concatenate([momentum, induction]) * weight).astype(jnp.bfloat16)
    returned = jnp.einsum(
        "cqrk,xabsk->cxabsqr", products, anal_table, preferred_element_type=jnp.float32
    ).astype(jnp.bfloat16)
    returned = returned.reshape(6, 2, ang_count, piece_len)
    gathered = lax.all_to_all(
        lax.all_to_all(returned, "rad", split_axis=3, concat_axis=3, tiled=True),
        "ang",
        split_axis=2,
        concat_axis=2,
        tiled=True,
    )
    gathered = gathered.reshape(6, 2, ang_count, rad_count, slots_here, band_rows, shell_rows)
    gathered = jnp.transpose(gathered, (0, 1, 4, 2, 5, 3, 6)).reshape(
        6, 2, slots_here, half_lat, 2, shells
    )
    northern = gathered[:, :, :, :, 0].astype(jnp.float32)
    southern = gathered[:, :, :, :, 1].astype(jnp.float32)
    hemi_sum = (northern + southern).astype(jnp.bfloat16)
    hemi_diff = (northern - southern).astype(jnp.bfloat16)
    coef_even = jnp.einsum(
        "cxstr,stn->cxsnr", hemi_sum, masked_rows[:, :, 0::2], preferred_element_type=jnp.float32
    )
    coef_odd = jnp.einsum(
        "cxstr,stn->cxsnr", hemi_diff, masked_rows[:, :, 1::2], preferred_element_type=jnp.float32
    )
    nonlinear = (
        jnp.stack([coef_even, coef_odd], axis=4)
        .reshape(6, 2, slots_here, degrees, shells)
        .astype(jnp.bfloat16)
    )
    joined = jnp.concatenate([current, nonlinear], axis=4).reshape(
        2, 3, 2, slots_here, degrees, 2 * shells
    )
    stepped = jnp.einsum(
        "fkxsnq,frq->fkxsnr", joined, radial_ops, preferred_element_type=jnp.float32
    )
    stepped = stepped.reshape(6, 2, slots_here, degrees, shells)
    current = (stepped * damping[None, None, :, :, None]).astype(jnp.bfloat16)
    return current


def solution(mesh):
    placed = (
        P(None, None, ("rad", "ang"), None, None),
        P(("rad", "ang"), None, None),
        P(),
        P(None, "ang", "rad", None),
        P(None, "ang", "rad", None),
        P(),
        P(),
    )
    return jax.shard_map(
        per_device,
        mesh=mesh,
        in_specs=placed,
        out_specs=P(None, None, ("rad", "ang"), None, None),
        check_vma=False,
    )
```

profile of v0, /device:TPU:1, one launch (start us, length us, event | category | flops | bytes accessed | tf_op | source)
XLA Modules:
  0.0 501.2 jit_solution(15314463703196608412)
XLA Ops:
  0.0 0.8 iota_compare_fusion
  0.8 0.7 broadcast_select_fusion
  2.0 0.9 broadcast_multiply_fusion
  2.9 3.4 slice.50
  6.4 3.3 slice.48
  9.7 6.4 %slice.51 = bf16[6,2,2,128,128]{4,3,2,1,0:T(8,128)(2,1)S(1)} slice(bf16[6,2,2,256,128]{4,3,2,1,0:T(8,128)(2,1)} %param.7), slice={[0:6:1], [0:2:1], [0:2:1], [1:256:2], [0:128:1]} | slice | bytes 1572864 | tf_op jit(solution)/shard_map/slice | solution.py:96
  16.1 0.7 slice.49
  16.7 0.5 fusion.32
  17.2 0.5 fusion.23
  18.0 2.4 copy.39
  20.4 15.6 %convert_element_type.113 = bf16[6,2,2,64,6,8,16]{6,5,4,3,2,1,0:T(8,128)(2,1)} reshape(bf16[6,2,2,192,2,128]{5,4,3,2,1,0:T(2,128)(2,1)S(1)} %copy.39) | data formatting | bytes 4718592 | tf_op jit(solution)/shard_map/convert_element_type | solution.py:103
  36.1 17.5 %copy.40 = bf16[6,2,64,8,2,6,16]{2,6,5,4,3,1,0:T(8,128)(2,1)} copy(bf16[6,2,64,8,2,6,16]{6,3,5,2,4,1,0:T(8,128)(2,1)} %bitcast.95) | data formatting | bytes 4718592 | tf_op jit(solution)/shard_map/transpose | solution.py:104
  53.6 10.0 %copy.94 = bf16[6,2,64,1536]{2,1,0,3:T(2,128)(2,1)} copy(bf16[6,2,64,1536]{2,3,1,0:T(8,128)(2,1)} %bitcast.101) | data formatting | bytes 4718592 | tf_op jit(solution)/shard_map/reshape | solution.py:104
  63.6 6.7 %reshape.402 = bf16[8,2,73728]{2,1,0:T(2,128)(2,1)S(1)} reshape(bf16[1536,6,2,64]{3,2,1,0:T(2,128)(2,1)} %bitcast.97) | data formatting | bytes 4718592
  70.3 61.3 %all_to_all.20 = bf16[8,2,73728]{2,1,0:T(2,128)(2,1)} all-to-all(bf16[8,2,73728]{2,1,0:T(2,128)(2,1)S(1)} %reshape.402), channel_id=1, replica_groups=mesh['rad'=8,'ang'=64] {'rad'}, dimensions={0} | all-to-all | bytes 4718592 | tf_op jit(solution)/shard_map/all_to_all | solution.py:106
  131.6 7.7 %reshape.403 = bf16[1536,6,2,64]{3,2,1,0:T(2,128)(2,1)} reshape(bf16[8,2,73728]{2,1,0:T(2,128)(2,1)} %all_to_all.20) | data formatting | bytes 4718592
  139.3 12.5 %copy.42 = bf16[6,2,64,1536]{3,1,0,2:T(2,128)(2,1)} copy(bf16[6,2,64,1536]{2,1,0,3:T(2,128)(2,1)} %bitcast.98) | data formatting | bytes 4718592 | tf_op jit(solution)/shard_map/all_to_all | solution.py:106
  151.8 18.0 %all-to-all-start.1 = ((bf16[6,2,64,1536]{3,1,0,2:T(2,128)(2,1)}), bf16[6,2,64,1536]{3,1,0,2:T(2,128)(2,1)}, u32[]{:S(2)}, u32[]{:S(2)}) async-start(bf16[6,2,64,1536]{3,1,0,2:T(2,128)(2,1)} %copy.42), calls=%async_computation.1 | async-start | bytes 4718592 | tf_op jit(solution)/shard_map/all_to_all | solution.py:105
  170.4 1.2 broadcast_add_fusion
  171.6 16.7 %fusion.15 = (f32[1,64,8,2,1024]{4,1,3,0,2:T(8,128)S(1)}, f32[1,64,8,2,1024]{4,1,3,0,2:T(8,128)S(1)}) fusion(s32[64,8,2]{0,2,1:T(2,128)S(1)} %bitcast.106), kind=kLoop, calls=%fused_computation.32 | loop fusion | flops 15728640 | bytes 8392704 | tf_op jit(solution)/shard_map/cos | solution.py:25
  188.3 1.9 copy-done.1
  190.3 1.4 copy-done.2
  191.6 2.3 fusion.5
  193.9 32.2 %all-to-all-done.1 = bf16[6,2,64,1536]{3,1,0,2:T(2,128)(2,1)} async-done(((bf16[6,2,64,1536]{3,1,0,2:T(2,128)(2,1)}), bf16[6,2,64,1536]{3,1,0,2:T(2,128)(2,1)}, u32[]{:S(2)}, u32[]{:S(2)}) %all-to-all-start.1) | async-done | bytes 2359328 | tf_op jit(solution)/shard_map/all_to_all | solution.py:105
  226.2 7.8 %copy.43 = bf16[6,2,64,1536]{2,3,1,0:T(8,128)(2,1)} copy(bf16[6,2,64,1536]{3,1,0,2:T(2,128)(2,1)} %all-to-all-done.1) | data formatting | bytes 4718592 | tf_op jit(solution)/shard_map/all_to_all | solution.py:105
  233.9 6.7 %fusion.16 = f32[6,6,16,1024]{3,2,1,0:T(8,128)S(1)} fusion(f32[1,64,8,2,1024]{4,1,3,0,2:T(8,128)} %copy-done.2, f32[1,64,8,2,1024]{4,1,3,0,2:T(8,128)} %copy-done.1, bf16[6,2,64,8,2,6,16]{2,6,5,4,3,1,0:T(8,128)(2,1)} %bitcast.105), kind=kOutput, calls=%fused_computation.33 | convolution fusion | flops 2422210560 | bytes 13107200 | tf_op jit(solution)/shard_map/cxabsqr,xabsk->cqrk/dot_general | solution.py:113
  240.7 0.4 multiply_subtract_fusion.8
  241.3 1.0 copy-done.5
  243.3 1.7 copy-done.6
  245.0 23.1 %convert_bitcast_fusion = bf16[6,2,64,8,2,6,16]{6,3,5,0,4,2,1:T(8,128)(2,1)} fusion(bf16[2,64,8,2,1024,1,1]{4,1,3,0,2,6,5:T(8,128)(2,1)S(1)} %copy-done.6, f32[3,6,16,1024]{3,2,1,0:T(8,128)S(1)} %maximum_add_fusion.1, f32[3,6,16,1024]{3,2,1,0:T(8,128)S(1)} %maximum_add_fusion, f32[6]{0:T(128)S(1)} %sine_multiply_fusion), kind=kOutput, calls=%fused_computation | convolution fusion | flops 2418868224 | bytes 8912920 | tf_op jit(solution)/shard_map/cqrk,xabsk->cxabsqr/dot_general | solution.py:119
  268.1 17.6 %copy.46 = bf16[6,2,64,8,2,6,16]{2,6,5,4,3,1,0:T(8,128)(2,1)} copy(bf16[6,2,64,8,2,6,16]{6,3,5,0,4,2,1:T(8,128)(2,1)} %convert_bitcast_fusion) | data formatting | bytes 4718592 | tf_op jit(solution)/shard_map/convert_element_type | solution.py:121
  285.7 10.0 %copy.93 = bf16[6,2,64,1536]{2,1,0,3:T(2,128)(2,1)} copy(bf16[6,2,64,1536]{2,3,1,0:T(8,128)(2,1)} %bitcast.102) | data formatting | bytes 4718592 | tf_op jit(solution)/shard_map/reshape | solution.py:122
  295.6 6.7 %reshape.404 = bf16[8,2,73728]{2,1,0:T(2,128)(2,1)S(1)} reshape(bf16[1536,6,2,64]{3,2,1,0:T(2,128)(2,1)} %bitcast.99) | data formatting | bytes 4718592
  302.4 60.5 %all_to_all.21 = bf16[8,2,73728]{2,1,0:T(2,128)(2,1)} all-to-all(bf16[8,2,73728]{2,1,0:T(2,128)(2,1)S(1)} %reshape.404), channel_id=1, replica_groups=mesh['rad'=8,'ang'=64] {'rad'}, dimensions={0} | all-to-all | bytes 4718592 | tf_op jit(solution)/shard_map/all_to_all | solution.py:124
  362.9 7.7 %reshape.405 = bf16[1536,6,2,64]{3,2,1,0:T(2,128)(2,1)} reshape(bf16[8,2,73728]{2,1,0:T(2,128)(2,1)} %all_to_all.21) | data formatting | bytes 4718592
  370.6 12.5 %copy.48 = bf16[6,2,64,1536]{3,1,0,2:T(2,128)(2,1)} copy(bf16[6,2,64,1536]{2,1,0,3:T(2,128)(2,1)} %bitcast.100) | data formatting | bytes 4718592 | tf_op jit(solution)/shard_map/all_to_all | solution.py:124
  383.0 6.0 %all-to-all-start.3 = ((bf16[6,2,64,1536]{3,1,0,2:T(2,128)(2,1)}), bf16[6,2,64,1536]{3,1,0,2:T(2,128)(2,1)S(1)}, u32[]{:S(2)}, u32[]{:S(2)}) async-start(bf16[6,2,64,1536]{3,1,0,2:T(2,128)(2,1)} %copy.48), calls=%async_computation.3 | async-start | bytes 4718592 | tf_op jit(solution)/shard_map/all_to_all | solution.py:123
  389.1 56.4 %all-to-all-done.3 = bf16[6,2,64,1536]{3,1,0,2:T(2,128)(2,1)S(1)} async-done(((bf16[6,2,64,1536]{3,1,0,2:T(2,128)(2,1)}), bf16[6,2,64,1536]{3,1,0,2:T(2,128)(2,1)S(1)}, u32[]{:S(2)}, u32[]{:S(2)}) %all-to-all-start.3) | async-done | bytes 2359328 | tf_op jit(solution)/shard_map/all_to_all | solution.py:123
  445.5 5.6 %copy.49 = bf16[6,2,64,1536]{2,3,1,0:T(8,128)(2,1)} copy(bf16[6,2,64,1536]{3,1,0,2:T(2,128)(2,1)S(1)} %all-to-all-done.3) | data formatting | bytes 4718592 | tf_op jit(solution)/shard_map/all_to_all | solution.py:123
  451.1 16.4 %copy.50 = bf16[6,2,2,64,6,8,16]{6,5,4,3,2,1,0:T(8,128)(2,1)} copy(bf16[6,2,2,64,6,8,16]{3,6,4,2,5,1,0:T(8,128)(2,1)} %bitcast.103) | data formatting | bytes 4718592 | tf_op jit(solution)/shard_map/transpose | solution.py:131
  467.5 22.9 %reshape.389 = bf16[6,2,2,192,2,128]{5,4,3,2,1,0:T(2,128)(2,1)S(1)} reshape(bf16[6,2,2,64,6,8,16]{6,5,4,3,2,1,0:T(8,128)(2,1)} %copy.50) | data formatting | bytes 4718592 | tf_op jit(solution)/shard_map/reshape | solution.py:131
  490.4 4.9 add_convert_fusion
  495.3 0.4 fusion.21
  495.7 0.4 fusion.22
  496.3 1.6 copy.53
  497.9 0.4 pad_maximum_fusion.1
  498.4 1.0 fusion.36
  499.3 1.6 fusion.13
  (34 shorter events, 2.7 us)
Async XLA Ops:
  0.0 498.4 %copy-start = (bf16[2,128,256]{2,1,0:T(8,128)(2,1)S(1)}, bf16[2,128,256]{2,1,0:T(8,128)(2,1)}, u32[]{:S(2)}) copy-start(bf16[2,128,256]{2,1,0:T(8,128)(2,1)} %param.9) | copy-start | bytes 393220
  0.0 16.0 %copy-start.3 = (bf16[6,2,2,256,128]{4,3,2,1,0:T(8,128)(2,1)S(1)}, bf16[6,2,2,256,128]{4,3,2,1,0:T(8,128)(2,1)}, u32[]{:S(2)}) copy-start(bf16[6,2,2,256,128]{4,3,2,1,0:T(8,128)(2,1)} %param.7) | copy-start | bytes 4718596
  151.8 18.1 %copy-start.8 = (bf16[3,6,16,1024]{3,2,1,0:T(8,128)(2,1)S(1)}, bf16[3,6,16,1024]{3,2,1,0:T(8,128)(2,1)}, u32[]{:S(2)}) copy-start(bf16[3,6,16,1024]{3,2,1,0:T(8,128)(2,1)} %param.11) | copy-start | bytes 1769476
  151.8 18.2 %copy-start.7 = (bf16[3,6,16,1024]{3,2,1,0:T(8,128)(2,1)S(1)}, bf16[3,6,16,1024]{3,2,1,0:T(8,128)(2,1)}, u32[]{:S(2)}) copy-start(bf16[3,6,16,1024]{3,2,1,0:T(8,128)(2,1)} %param.10) | copy-start | bytes 1769476
  151.8 74.4 %all-to-all-start.1 = ((bf16[6,2,64,1536]{3,1,0,2:T(2,128)(2,1)}), bf16[6,2,64,1536]{3,1,0,2:T(2,128)(2,1)}, u32[]{:S(2)}, u32[]{:S(2)}) async-start(bf16[6,2,64,1536]{3,1,0,2:T(2,128)(2,1)} %copy.42), calls=%async_computation.1 | async-start | bytes 4718592 | tf_op jit(solution)/shard_map/all_to_all | solution.py:105
  188.3 1.9 copy-start.1
  188.3 3.3 copy-start.2
  241.1 1.3 copy-start.5
  242.8 2.2 copy-start.6
  383.0 62.5 %all-to-all-start.3 = ((bf16[6,2,64,1536]{3,1,0,2:T(2,128)(2,1)}), bf16[6,2,64,1536]{3,1,0,2:T(2,128)(2,1)S(1)}, u32[]{:S(2)}, u32[]{:S(2)}) async-start(bf16[6,2,64,1536]{3,1,0,2:T(2,128)(2,1)} %copy.48), calls=%async_computation.3 | async-start | bytes 4718592 | tf_op jit(solution)/shard_map/all_to_all | solution.py:123
  496.3 1.6 copy-start.4
where the time goes:
time: 510 us; the launch traced here: 501 us
  local copies, waits for them, and re-layouts  202 us (40%)
  blocking collectives  122 us (24%)
  waiting for transfers between devices  88.7 us (17%)
  matrix products  32.6 us (6%)
  other arithmetic  32.1 us (6%)
  starting transfers between devices  24 us (5%)
    all_to_all x1, blocking collectives, per_device(): lax.all_to_all(grid_vals, 'rad', split_axis=3, concat_axis=3, tiled=True)  61.3 us
    all_to_all x1, blocking collectives, per_device(): lax.all_to_all(returned, 'rad', split_axis=3, concat_axis=3, tiled=True)  60.5 us
    all_to_all x1, waiting for transfers between devices, per_device(): lax.all_to_all(lax.all_to_all(returned, 'rad', split_axis=3, concat_axis=...  56.4 us
    unnamed x22, local copies, waits for them, and re-layouts  34.9 us
    all_to_all x1, waiting for transfers between devices, per_device(): lax.all_to_all(lax.all_to_all(grid_vals, 'rad', split_axis=3, concat_axis...  32.2 us
    dot_general x1, matrix products, per_device(): jnp.einsum('cqrk,xabsk->cxabsqr', products, anal_table, preferred_element...  23.1 us
    reshape x1, local copies, waits for them, and re-layouts, per_device(): jnp.transpose(gathered, (0, 1, 4, 2, 5, 3, 6))  22.9 us
    all_to_all x1, starting transfers between devices, per_device(): lax.all_to_all(lax.all_to_all(grid_vals, 'rad', split_axis=3, concat_axis...  18 us
  transfers between devices with their start and end apart: 2, of which 2 were waited for; matrix products, arithmetic and copies ran while one was open for 4% of the time, Pallas kernels for 0%

commit v1 on v0

v1 whole, which is shorter than its diff:
```python
import functools
import math

import jax
import jax.numpy as jnp
from jax import lax
from jax.experimental import pallas as pl
from jax.experimental.pallas import tpu as pltpu
from jax.sharding import PartitionSpec as P

F32 = jnp.float32
BF16 = jnp.bfloat16
MESH = pl.DeviceIdType.MESH

NX = 4
NZ = 16
NY = 8
NC = 3
NG = 3
STAGES = 6
coriolis = 3.0


def iota(shape, axis):
    return lax.broadcasted_iota(jnp.int32, shape, axis)


def dot(a, b, dims=((1,), (0,))):
    return lax.dot_general(a, b, (dims, ((), ())), preferred_element_type=F32)


def kernel(
    assign_ref,
    counts_ref,
    pair_ref,
    state_ref,
    leg_ref,
    ops_ref,
    flow_ref,
    mag_ref,
    out_ref,
    swap,
    turn,
    leg_fwd,
    leg_back,
    coeffs,
    table,
    table_back,
    lhs,
    fields,
    prods,
    xs,
    xr,
    ys,
    yr,
    zs,
    zr,
    zbs,
    zbr,
    ybs,
    ybr,
    xbr,
    xsem,
    ysem,
    zsem,
    zbsem,
    ybsem,
    xbsem,
    lsem,
):
    my = lax.axis_index("rad")
    ang = lax.axis_index("ang")
    mx = ang // NZ
    mz = ang % NZ
    upper = mx // 2
    device = my * (NX * NZ) + ang

    def at_x(x):
        return (my, x * NZ + mz)

    def at_y(y):
        return (y, ang)

    def at_z(z):
        return (my, mx * NZ + z)

    barrier = pltpu.get_barrier_semaphore()

    @pl.loop(1, NX)
    def _(d):
        pl.semaphore_signal(barrier, inc=1, device_id=at_x((mx + d) % NX), device_id_type=MESH)

    @pl.loop(1, NY)
    def _(d):
        pl.semaphore_signal(barrier, inc=1, device_id=at_y((my + d) % NY), device_id_type=MESH)

    @pl.loop(1, NZ)
    def _(d):
        pl.semaphore_signal(barrier, inc=1, device_id=at_z((mz + d) % NZ), device_id_type=MESH)

    def remote(src, dst, sems, i, d, target):
        return pltpu.make_async_remote_copy(
            src_ref=src,
            dst_ref=dst,
            send_sem=sems.at[0, i, d],
            recv_sem=sems.at[1, i, d],
            device_id=target,
            device_id_type=MESH,
        )

    def x_copy(i, d):
        x = (mx + d) % NX
        return remote(xs.at[i, x], xr.at[i, mx], xsem, i, d, at_x(x))

    def y_copy(i, d):
        y = (my + d) % NY
        return remote(ys.at[i, y], yr.at[i, my], ysem, i, d, at_y(y))

    def z_copy(i, d):
        z = (mz + d) % NZ
        return remote(zs.at[i, z], zr.at[i, mz], zsem, i, d, at_z(z))

    def zb_copy(i, d):
        z = (mz + d) % NZ
        return remote(zbs.at[i, z], zbr.at[i, mz], zbsem, i, d, at_z(z))

    def yb_copy(i, d):
        y = (my + d) % NY
        return remote(ybs.at[i, y], ybr.at[i, my], ybsem, i, d, at_y(y))

    def xb_copy(i, d):
        x = (mx + d) % NX
        return remote(ybr.at[i, :, x % 2], xbr.at[i, mx], xbsem, i, d, at_x(x))

    def own(k, i):
        src, dst = (
            (xs.at[i, mx], xr.at[i, mx]),
            (ys.at[i, my], yr.at[i, my]),
            (zs.at[i, mz], zr.at[i, mz]),
            (zbs.at[i, mz], zbr.at[i, mz]),
            (ybs.at[i, my], ybr.at[i, my]),
            (ybr.at[i, :, mx % 2], xbr.at[i, mx]),
        )[k]
        return pltpu.make_async_copy(src, dst, lsem.at[k, i])

    copies = (x_copy, y_copy, z_copy, zb_copy, yb_copy, xb_copy)
    sizes = (NX, NY, NZ, NZ, NY, NX)

    def send(k, i):
        own(k, i).start()

        @pl.loop(1, sizes[k])
        def _(d):
            copies[k](i, d).start()

    def receive(k, i):
        @pl.loop(1, sizes[k])
        def _(d):
            copies[k](i, d).wait_recv()

        own(k, i).wait()

    def slot(pos):
        return (1 - upper) * pos + upper * (1 - pos)

    @pl.loop(0, 4)
    def _(b):
        row = iota((256, 1024), 0) + b * 256
        col = iota((256, 1024), 1)
        image = (row % 128) // 16 * 128 + row // 128 * 16 + row % 16
        swap[pl.ds(pl.multiple_of(b * 256, 256), 256), :] = jnp.where(col == image, 1.0, 0.0).astype(BF16)

    def masks(pos):
        s = slot(pos)
        live = s < counts_ref[device]
        order = jnp.where(live, assign_ref[device * 2 + s], 0)
        top = jnp.where(live, 511 - order, -1)
        return order, top

    for pos in range(2):
        _, top = masks(pos)
        rows = leg_ref[slot(pos)]
        rows = jnp.where(iota((192, 256), 1) <= top, rows.astype(F32), 0.0).astype(BF16)
        for i in range(NC):
            r = iota((128, 192), 0)
            pick = jnp.where(iota((128, 192), 1) == 3 * (r // 32 * 16 + r % 16) + i, 1.0, 0.0).astype(BF16)
            picked = dot(pick, rows)
            odd_n = iota((128, 256), 1) % 2
            south = iota((128, 256), 0) // 16 % 2
            leg_fwd[i, pos * 128 : (pos + 1) * 128, :] = jnp.where(odd_n * south == 1, -picked, picked).astype(BF16)
            kept = jnp.where(odd_n == south, picked, 0.0)
            leg_back[pos, :, i * 128 : (i + 1) * 128] = kept.T.astype(BF16)

    for g in range(NG):
        joined = jnp.concatenate(
            [state_ref[2 * g + cc, x, slot(pos)] for pos in range(2) for x in range(2) for cc in range(2)], axis=1
        )
        for b in range(4):
            coeffs[g, :, b * 256 : (b + 1) * 256] = dot(joined, swap[:, b * 256 : (b + 1) * 256]).astype(BF16)

    first = iota((128, 256), 1) % 128 < 64

    def synthesis(i):
        @pl.loop(0, NG)
        def _(g):
            for b in range(4):
                both = dot(leg_fwd[i], coeffs[g, :, b * 256 : (b + 1) * 256])
                grid = jnp.where(first, both[:128], both[128:]).astype(BF16)
                xs[i, :, g, :, b * 256 : (b + 1) * 256] = grid.reshape(NX, 32, 256)

    synthesis(0)
    pl.semaphore_wait(barrier, NX + NY + NZ - 3)
    send(0, 0)

    @pl.loop(1, NC)
    def _(i):
        synthesis(i)
        send(0, i)

    a = iota((512, 512), 0)
    b = iota((512, 512), 1)
    image = (a % 16) * 32 + a // 16 % 2 * 16 + a // 32
    turn[...] = jnp.where(b == image, 1.0, 0.0).astype(BF16)

    scale = 1.0 / math.sqrt(512)
    for pos in range(2):
        m = pair_ref[:, pos : pos + 1]
        lane = iota((256, 128), 1)
        fine = (m * lane & 1023).astype(F32) * (2.0 * math.pi / 1024)
        cos_fine = jnp.cos(fine) * scale
        sin_fine = jnp.sin(fine) * scale
        coarse = (m * lane & 7).astype(F32) * (2.0 * math.pi / 8)
        cos_coarse = jnp.cos(coarse)
        sin_coarse = jnp.sin(coarse)
        back = jnp.where(m == 0, 0.5, 1.0)
        for k in range(8):
            ck = cos_coarse[:, k : k + 1]
            sk = sin_coarse[:, k : k + 1]
            re = (cos_fine * ck - sin_fine * sk).astype(BF16)
            im = (-(sin_fine * ck + cos_fine * sk)).astype(BF16)
            lanes = slice(k * 128, (k + 1) * 128)
            table[pos * 512 : pos * 512 + 256, lanes] = re
            table[pos * 512 + 256 : pos * 512 + 512, lanes] = im
            table_back[pos * 512 : pos * 512 + 256, lanes] = (re.astype(F32) * back).astype(BF16)
            table_back[pos * 512 + 256 : pos * 512 + 512, lanes] = (im.astype(F32) * back).astype(BF16)

    def fold(i):
        receive(0, i)
        for p in range(2):
            for g in range(NG):
                pair = xr[i, p, g] + xr[i, p + 2, g]
                for y in range(NY):
                    ys[i, y, g, p] = pair[:, y * 128 : (y + 1) * 128]
        send(1, i)

    def spread(i):
        receive(1, i)
        rows = jnp.concatenate([yr[i, :, g].reshape(512, 128) for g in range(NG)], axis=1)
        turned = dot(turn[...], rows).astype(BF16)
        for g in range(NG):
            zs[i, :, g] = turned[:, g * 128 : (g + 1) * 128].reshape(NZ, 32, 128)
        send(2, i)

    def physics(i):
        receive(2, i)
        for g in range(NG):
            for h in range(2):
                block = zr[i, :, g, h * 16 : (h + 1) * 16, :].reshape(256, 128).T
                for p in range(4):
                    row = h * 96 + g * 32
                    lhs[row : row + 32, p * 256 : (p + 1) * 256] = block[p * 32 : (p + 1) * 32]

        @pl.loop(0, 4)
        def _(b):
            lanes = pl.ds(pl.multiple_of(b * 256, 256), 256)
            fields[:, lanes] = dot(lhs[...], table[:, lanes])

        row_t = (iota((8, 128), 0) * 0 + ang * NC + i).astype(F32)
        north = (row_t + 0.5) * (math.pi / 384)
        for h in range(2):
            colat = math.pi - north if h == 1 else north
            along = (coriolis * jnp.cos(colat))[0:1, 0:1]
            across = (-coriolis * jnp.sin(colat))[0:1, 0:1]
            weight = (math.pi / 2 * jnp.sin(colat))[0:1, 0:1]

            @pl.loop(0, 4)
            def _(b):
                lanes = pl.ds(pl.multiple_of(b * 256, 256), 256)
                u = [fields[h * 96 + c * 16 : h * 96 + (c + 1) * 16, lanes] for c in range(3)]
                v = [fields[h * 96 + (c + 3) * 16 : h * 96 + (c + 4) * 16, lanes] for c in range(3)]
                w = [flow_ref[c, 2 * i + h, :, lanes].astype(F32) for c in range(3)]
                f = [mag_ref[c, 2 * i + h, :, lanes].astype(F32) for c in range(3)]
                spin = [w[0] + along, w[1] + across, w[2]]
                for c in range(3):
                    n, o = (c + 1) % 3, (c + 2) % 3
                    momentum = (u[n] * spin[o] - u[o] * spin[n]) + (f[n] * v[o] - f[o] * v[n])
                    induction = (u[n] * f[o] - u[o] * f[n]) + (w[n] * v[o] - w[o] * v[n])
                    row = h * 96 + c * 16
                    prods[row : row + 16, lanes] = (momentum * weight).astype(BF16)
                    prods[row + 48 : row + 64, lanes] = (induction * weight).astype(BF16)

        @pl.loop(0, 4)
        def _(p):
            returned = dot(prods[...], table_back[pl.ds(pl.multiple_of(p * 256, 256), 256), :], ((1,), (1,)))
            returned = returned.astype(BF16).astype(F32)
            n, s = returned[:96], returned[96:]
            fields[0:96, pl.ds(pl.multiple_of(p * 256, 256), 256)] = n + s
            fields[96:192, pl.ds(pl.multiple_of(p * 256, 256), 256)] = n - s

        for g in range(NG):
            for h in range(2):
                row = h * 96 + g * 32
                block = jnp.concatenate([fields[row : row + 32, p * 256 : (p + 1) * 256] for p in range(4)], axis=0)
                zbs[i, :, g, h * 16 : (h + 1) * 16, :] = block.T.astype(BF16).reshape(NZ, 16, 128)
        send(3, i)

    def gather(i):
        receive(3, i)
        rows = jnp.concatenate([zbr[i, :, g].reshape(512, 128) for g in range(NG)], axis=1)
        turned = dot(turn[...], rows).astype(BF16)
        for g in range(NG):
            block = turned[:, g * 128 : (g + 1) * 128].reshape(NY, 2, 32, 128)
            for p in range(2):
                ybs[i, :, p, g] = block[:, p]
        send(4, i)

    def unfold(i):
        receive(4, i)
        send(5, i)

    stages = (fold, spread, physics, gather, unfold, functools.partial(receive, 5))

    @pl.loop(0, NC + STAGES - 1)
    def _(step):
        for k, stage in enumerate(stages):

            @pl.when(jnp.logical_and(step >= k, step < k + NC))
            def _():
                stage(step - k)

    @pl.loop(0, NG)
    def _(g):
        halves = []
        for b in range(4):
            rows = jnp.concatenate([xbr[:, :, 2 * b + e, g].reshape(384, 128) for e in range(2)], axis=1)
            halves.append(jnp.where(iota((256, 256), 1) % 128 < 64, dot(leg_back[0], rows), dot(leg_back[1], rows)).astype(BF16))
        nonlinear = jnp.concatenate(halves, axis=1)
        for pos in range(2):
            order, top = masks(pos)
            n = iota((256, 128), 0)
            degree = (order + n).astype(F32)
            damping = jnp.where(n <= top, 1.0 / (1.0 + degree * (degree + 1.0) / 65536.0), 0.0)
            for x in range(2):
                j = pos * 4 + x * 2
                terms = dot(nonlinear, swap[:, j * 128 : (j + 2) * 128]).astype(BF16)
                for cc in range(2):
                    c = 2 * g + cc
                    joined = jnp.concatenate([state_ref[c, x, slot(pos)], terms[:, cc * 128 : (cc + 1) * 128]], axis=1)
                    stepped = dot(joined, ops_ref[c // 3], ((1,), (1,)))
                    out_ref[c, x, slot(pos)] = (stepped * damping).astype(BF16)

    for k in range(STAGES):

        @pl.loop(0, NC)
        def _(i):
            @pl.loop(1, sizes[k])
            def _(d):
                copies[k](i, d).wait_send()


def per_device(state, legendre, radial_ops, base_flow, base_field, assign, counts):
    live = jnp.arange(2, dtype=jnp.int32)[None, :] < counts[:, None]
    orders = jnp.where(live, assign, 0).reshape(NY, 2, 2, NZ, 2)
    pairs = orders[:, 0] + orders[:, 1, :, :, ::-1]
    pairs = jnp.transpose(pairs, (2, 0, 1, 3)).reshape(256, 2)
    vmem = pl.BlockSpec(memory_space=pltpu.VMEM)
    smem = pl.BlockSpec(memory_space=pltpu.SMEM)
    dma = pltpu.SemaphoreType.DMA
    return pl.pallas_call(
        kernel,
        out_shape=jax.ShapeDtypeStruct(state.shape, BF16),
        in_specs=[smem, smem] + [vmem] * 6,
        out_specs=vmem,
        scratch_shapes=[
            pltpu.VMEM((1024, 1024), BF16),
            pltpu.VMEM((512, 512), BF16),
            pltpu.VMEM((NC, 256, 256), BF16),
            pltpu.VMEM((2, 256, 384), BF16),
            pltpu.VMEM((NG, 256, 1024), BF16),
            pltpu.VMEM((1024, 1024), BF16),
            pltpu.VMEM((1024, 1024), BF16),
            pltpu.VMEM((192, 1024), BF16),
            pltpu.VMEM((192, 1024), F32),
            pltpu.VMEM((192, 1024), BF16),
            pltpu.VMEM((NC, NX, NG, 32, 1024), BF16),
            pltpu.VMEM((NC, NX, NG, 32, 1024), BF16),
            pltpu.VMEM((NC, NY, NG, 2, 32, 128), BF16),
            pltpu.VMEM((NC, NY, NG, 2, 32, 128), BF16),
            pltpu.VMEM((NC, NZ, NG, 32, 128), BF16),
            pltpu.VMEM((NC, NZ, NG, 32, 128), BF16),
            pltpu.VMEM((NC, NZ, NG, 32, 128), BF16),
            pltpu.VMEM((NC, NZ, NG, 32, 128), BF16),
            pltpu.VMEM((NC, NY, 2, NG, 32, 128), BF16),
            pltpu.VMEM((NC, NY, 2, NG, 32, 128), BF16),
            pltpu.VMEM((NC, NX, NY, NG, 32, 128), BF16),
            dma((2, NC, NX)),
            dma((2, NC, NY)),
            dma((2, NC, NZ)),
            dma((2, NC, NZ)),
            dma((2, NC, NY)),
            dma((2, NC, NX)),
            dma((STAGES, NC)),
        ],
        compiler_params=pltpu.CompilerParams(
            collective_id=0, has_side_effects=True, vmem_limit_bytes=56 * 1024 * 1024
        ),
    )(assign.reshape(-1), counts, pairs, state, legendre, radial_ops, base_flow, base_field)


def solution(mesh):
    placed = (
        P(None, None, ("rad", "ang"), None, None),
        P(("rad", "ang"), None, None),
        P(),
        P(None, "ang", "rad", None),
        P(None, "ang", "rad", None),
        P(),
        P(),
    )
    return jax.shard_map(
        per_device,
        mesh=mesh,
        in_specs=placed,
        out_specs=P(None, None, ("rad", "ang"), None, None),
        check_vma=False,
    )
```

time: 510 us -> 135 us (0.26); the launches traced: 501 us -> 135 us
  local copies, waits for them, and re-layouts: 202 us -> 5.1 us
  Pallas kernels: 0 us -> 128 us
  blocking collectives: 122 us -> 0 us
  waiting for transfers between devices: 88.7 us -> 0 us
  matrix products: 32.6 us -> 0 us
  other arithmetic: 32.1 us -> 1.43 us
  starting transfers between devices: 24 us -> 0 us
    pallas_call x0 -> x1, Pallas kernels: none -> 128 us  [per_device(): pl.pallas_call(kernel, out_shape=jax.ShapeDtypeStruct(state.shape, BF16),...]
    all_to_all x2 -> x0, blocking collectives: 122 us -> none  [the longest x1 61.3 us: per_device(): lax.all_to_all(grid_vals, 'rad', split_axis=3, concat_axis=3, tiled=True)]
    all_to_all x2 -> x0, waiting for transfers between devices: 88.7 us -> none  [the longest x1 56.4 us: per_device(): lax.all_to_all(lax.all_to_all(returned, 'rad', split_axis=3, concat_axis=...]
    reshape x5 -> x2, local copies, waits for them, and re-layouts: 42.9 us -> 0.87 us  [the longest x1 0.77 us: per_device(): assign.reshape(-1)]
    all_to_all x4 -> x0, local copies, waits for them, and re-layouts: 38.3 us -> none  [the longest x1 12.5 us: per_device(): lax.all_to_all(grid_vals, 'rad', split_axis=3, concat_axis=3, tiled=True)]
    transpose x2 -> x0, local copies, waits for them, and re-layouts: 33.9 us -> none  [the longest x1 17.5 us: per_device(): jnp.transpose(grid_vals, (0, 1, 3, 5, 2, 4, 6))]
    convert_element_type x2 -> x0, local copies, waits for them, and re-layouts: 33.2 us -> none  [the longest x1 17.6 us: per_device(): returned = jnp.einsum('cqrk,xabsk->cxabsqr', products, anal_table, prefer...]
    dot_general x7 -> x0, matrix products: 32.6 us -> none  [the longest x1 23.1 us: per_device(): jnp.einsum('cqrk,xabsk->cxabsqr', products, anal_table, preferred_element...]
  transfers between devices with their start and end apart: 2 -> 0, of which waited for: 2 -> 0; matrix products, arithmetic and copies ran while one was open for 4% -> 0% of each run, Pallas kernels for 0% -> 0%
where the time goes in v1:
time: 135 us
  Pallas kernels  128 us (95%)
  local copies, waits for them, and re-layouts  5.1 us (4%)
  other arithmetic  1.43 us (1%)
    pallas_call x1, Pallas kernels, per_device(): pl.pallas_call(kernel, out_shape=jax.ShapeDtypeStruct(state.shape, BF16),...  128 us
    unnamed x4, local copies, waits for them, and re-layouts  3.93 us

profile of v1, /device:TPU:1, one launch (start us, length us, event | category | flops | bytes accessed | tf_op | source)
XLA Modules:
  0.0 135.0 jit_solution(8109501150231119200)
XLA Ops:
  0.0 0.7 compare_select_fusion
  0.7 0.1 reshape.12
  0.8 0.2 copy.14
  1.0 0.3 rev.3
  1.3 0.2 copy.13
  1.5 0.7 add.6
  2.3 0.8 copy.10
  3.1 0.8 reshape.11.assign_ref
  3.9 128.4 %shard_map.73 = bf16[6,2,2,256,128]{4,3,2,1,0:T(8,128)(2,1)} custom-call(s32[1024]{0:T(1024)} %reshape.11.assign_ref, s32[512]{0:T(512)} %counts_ref.1, s32[256,2]{1,0:T(8,128)} %bitcast.7, bf16[6,2,2,256,128]{4,3,2,1,0:T(8,128)(2,1)} %state_ref.1, bf16[2,192,256]{2,1,0:T(8,128)(2,1)} %leg_ref.1, bf16[2,128,256]{2,1,0:T(8,128)(2,1)} %ops_ref.1, ...), custom_call_target="tpu_custom_call" | custom-call | tf_op jit(solution)/shard_map/pallas_call | solution.py:379
  132.3 2.7 %copy.16 = bf16[6,2,2,256,128]{4,3,2,1,0:T(8,128)(2,1)} copy(bf16[6,2,2,256,128]{4,3,2,1,0:T(8,128)(2,1)} %shard_map.73) | data formatting | bytes 3145728
  (1 shorter events, 0.0 us)

commit v2 on v1

v2 whole, which is shorter than its diff:
```python
import math

import jax
import jax.numpy as jnp
from jax import lax
from jax.experimental import pallas as pl
from jax.experimental.pallas import tpu as pltpu
from jax.sharding import PartitionSpec as P

F32 = jnp.float32
BF16 = jnp.bfloat16
MESH = pl.DeviceIdType.MESH

NX = 4
NZ = 16
NY = 8
NC = 3
NG = 3
NQ = NC * NG
coriolis = 3.0


def iota(shape, axis):
    return lax.broadcasted_iota(jnp.int32, shape, axis)


def dot(a, b, dims=((1,), (0,))):
    return lax.dot_general(a, b, (dims, ((), ())), preferred_element_type=F32)


def kernel(
    assign_ref,
    counts_ref,
    assign_rows_ref,
    counts_row_ref,
    leg_ref,
    ops_ref,
    state_ref,
    flow_ref,
    mag_ref,
    out_ref,
    state,
    flow,
    mag,
    out,
    swap,
    turn,
    leg_fwd,
    leg_back,
    coeffs,
    table,
    table_back,
    lhs,
    fields,
    prods,
    xs,
    xr,
    ys,
    yr,
    zs,
    zr,
    zbs,
    zbr,
    ybs,
    ybr,
    xbr,
    send_sems,
    recv_sems,
    own_sems,
    load_sems,
    store_sems,
):
    my = lax.axis_index("rad")
    ang = lax.axis_index("ang")
    mx = ang // NZ
    mz = ang % NZ
    upper = mx // 2
    device = my * (NX * NZ) + ang

    loads = [
        pltpu.make_async_copy(state_ref.at[2 * g : 2 * g + 2], state.at[2 * g : 2 * g + 2], load_sems.at[g])
        for g in range(NG)
    ]
    loads += [
        pltpu.make_async_copy(flow_ref, flow, load_sems.at[NG]),
        pltpu.make_async_copy(mag_ref, mag, load_sems.at[NG + 1]),
    ]
    stores = [
        pltpu.make_async_copy(out.at[2 * g : 2 * g + 2], out_ref.at[2 * g : 2 * g + 2], store_sems.at[g])
        for g in range(NG)
    ]
    for load in loads:
        load.start()

    def at_x(x):
        return (my, x * NZ + mz)

    def at_y(y):
        return (y, ang)

    def at_z(z):
        return (my, mx * NZ + z)

    barrier = pltpu.get_barrier_semaphore()

    @pl.loop(1, NX)
    def _(d):
        pl.semaphore_signal(barrier, inc=1, device_id=at_x((mx + d) % NX), device_id_type=MESH)

    @pl.loop(1, NY)
    def _(d):
        pl.semaphore_signal(barrier, inc=1, device_id=at_y((my + d) % NY), device_id_type=MESH)

    @pl.loop(1, NZ)
    def _(d):
        pl.semaphore_signal(barrier, inc=1, device_id=at_z((mz + d) % NZ), device_id_type=MESH)

    rings = (
        (NX, mx, at_x, lambda q, x: xs.at[q, x], lambda q: xr.at[q, mx], xr),
        (NY, my, at_y, lambda q, y: ys.at[q, y], lambda q: yr.at[q, my], yr),
        (NZ, mz, at_z, lambda q, z: zs.at[q, z], lambda q: zr.at[q, mz], zr),
        (NZ, mz, at_z, lambda q, z: zbs.at[q, z], lambda q: zbr.at[q, mz], zbr),
        (NY, my, at_y, lambda q, y: ybs.at[q, y], lambda q: ybr.at[q, my], ybr),
        (NX, mx, at_x, lambda q, x: ybr.at[q, :, x % 2], lambda q: xbr.at[q, mx], xbr),
    )

    def own(k, q):
        _, me, _, source, target, _ = rings[k]
        return pltpu.make_async_copy(source(q, me), target(q), own_sems.at[k, q])

    def send(k, q):
        size, me, where, source, target, _ = rings[k]
        own(k, q).start()

        @pl.loop(1, size)
        def _(d):
            place = (me + d) % size
            pltpu.make_async_remote_copy(
                src_ref=source(q, place),
                dst_ref=target(q),
                send_sem=send_sems.at[k],
                recv_sem=recv_sems.at[k, q],
                device_id=where(place),
                device_id_type=MESH,
            ).start()

    def others(k, q):
        size, me, where, _, _, landing = rings[k]
        region = landing.at[q, pl.ds(0, size - 1)]
        return pltpu.make_async_remote_copy(
            src_ref=region,
            dst_ref=region,
            send_sem=send_sems.at[k],
            recv_sem=recv_sems.at[k, q],
            device_id=where((me + 1) % size),
            device_id_type=MESH,
        )

    def receive(k, q):
        others(k, q).wait_recv()
        own(k, q).wait()

    def all_sent(k):
        size, me, where, _, _, landing = rings[k]
        region = landing.at[:, pl.ds(0, size - 1)]
        pltpu.make_async_remote_copy(
            src_ref=region,
            dst_ref=region,
            send_sem=send_sems.at[k],
            recv_sem=recv_sems.at[k, 0],
            device_id=where((me + 1) % size),
            device_id_type=MESH,
        ).wait_send()

    def slot(pos):
        return (1 - upper) * pos + upper * (1 - pos)

    def live_order(pos):
        s = slot(pos)
        live = s < counts_ref[device]
        order = jnp.where(live, assign_ref[s, device], 0)
        return order, jnp.where(live, 511 - order, -1)

    @pl.loop(0, 4)
    def _(b):
        row = iota((256, 1024), 0) + b * 256
        col = iota((256, 1024), 1)
        image = (row % 128) // 16 * 128 + row // 128 * 16 + row % 16
        swap[pl.ds(pl.multiple_of(b * 256, 256), 256), :] = jnp.where(col == image, 1.0, 0.0).astype(BF16)

    def legendre_rows(pos, i):
        _, top = live_order(pos)
        rows = leg_ref[slot(pos)]
        rows = jnp.where(iota((192, 256), 1) <= top, rows.astype(F32), 0.0).astype(BF16)
        r = iota((128, 192), 0)
        pick = jnp.where(iota((128, 192), 1) == 3 * (r // 32 * 16 + r % 16) + i, 1.0, 0.0).astype(BF16)
        picked = dot(pick, rows)
        odd_n = iota((128, 256), 1) % 2
        south = iota((128, 256), 0) // 16 % 2
        return picked, odd_n, south

    for i in range(NC):
        for pos in range(2):
            picked, odd_n, south = legendre_rows(pos, i)
            leg_fwd[i, pos * 128 : (pos + 1) * 128, :] = jnp.where(odd_n * south == 1, -picked, picked).astype(BF16)

    def shuffle(g):
        loads[g].wait()
        joined = jnp.concatenate(
            [state[2 * g + cc, x, slot(pos)] for pos in range(2) for x in range(2) for cc in range(2)], axis=1
        )
        for b in range(4):
            coeffs[g, :, b * 256 : (b + 1) * 256] = dot(joined, swap[:, b * 256 : (b + 1) * 256]).astype(BF16)

    def synthesis(q):
        first = iota((128, 256), 1) % 128 < 64
        for b in range(4):
            both = dot(leg_fwd[q // NG], coeffs[q % NG, :, b * 256 : (b + 1) * 256])
            grid = jnp.where(first, both[:128], both[128:]).astype(BF16)
            xs[q, :, :, b * 256 : (b + 1) * 256] = grid.reshape(NX, 32, 256)
        send(0, q)

    shuffle(0)
    pl.semaphore_wait(barrier, NX + NY + NZ - 3)
    synthesis(0)
    shuffle(1)
    synthesis(1)
    shuffle(2)
    synthesis(2)

    a = iota((512, 512), 0)
    b = iota((512, 512), 1)
    image = (a % 16) * 32 + a // 16 % 2 * 16 + a // 32
    turn[...] = jnp.where(b == image, 1.0, 0.0).astype(BF16)

    def transposed_legendre():
        for i in range(NC):
            for pos in range(2):
                picked, odd_n, south = legendre_rows(pos, i)
                kept = jnp.where(odd_n == south, picked, 0.0)
                leg_back[pos, :, i * 128 : (i + 1) * 128] = kept.T.astype(BF16)

    def tables():
        held = assign_rows_ref[...]
        held = jnp.where(iota((2, 512), 0) < counts_row_ref[...], held, 0)
        digits = jnp.concatenate([held >> 1, held & 1], axis=0).astype(F32).astype(BF16)
        place = iota((256, 512), 0)
        place = place // 2 % 8 * 64 + place % 2 * 16 + place // 16
        lane = iota((256, 512), 1)
        low = dot(jnp.where(lane == place, 1.0, 0.0).astype(BF16), digits, ((1,), (1,)))
        high = dot(jnp.where(lane == place + 32, 1.0, 0.0).astype(BF16), digits, ((1,), (1,)))
        scale = 1.0 / math.sqrt(512)
        for pos in range(2):
            m = 2.0 * (low[:, pos : pos + 1] + high[:, 1 - pos : 2 - pos]) + (
                low[:, 2 + pos : 3 + pos] + high[:, 3 - pos : 4 - pos]
            )
            m = m.astype(jnp.int32)
            lane = iota((256, 128), 1)
            fine = (m * lane & 1023).astype(F32) * (2.0 * math.pi / 1024)
            cos_fine = jnp.cos(fine) * scale
            sin_fine = jnp.sin(fine) * scale
            coarse = (m * lane & 7).astype(F32) * (2.0 * math.pi / 8)
            cos_coarse = jnp.cos(coarse)
            sin_coarse = jnp.sin(coarse)
            back = jnp.where(m == 0, 0.5, 1.0)
            for k in range(8):
                ck = cos_coarse[:, k : k + 1]
                sk = sin_coarse[:, k : k + 1]
                re = (cos_fine * ck - sin_fine * sk).astype(BF16)
                im = (-(sin_fine * ck + cos_fine * sk)).astype(BF16)
                lanes = slice(k * 128, (k + 1) * 128)
                table[pos * 512 : pos * 512 + 256, lanes] = re
                table[pos * 512 + 256 : pos * 512 + 512, lanes] = im
                table_back[pos * 512 : pos * 512 + 256, lanes] = (re.astype(F32) * back).astype(BF16)
                table_back[pos * 512 + 256 : pos * 512 + 512, lanes] = (im.astype(F32) * back).astype(BF16)

    def fold(q):
        receive(0, q)
        for p in range(2):
            pair = xr[q, p] + xr[q, p + 2]
            for y in range(NY):
                ys[q, y, p] = pair[:, y * 128 : (y + 1) * 128]
        send(1, q)

    def spread(q):
        receive(1, q)
        zs[q] = dot(turn[...], yr[q].reshape(512, 128)).astype(BF16).reshape(NZ, 32, 128)
        send(2, q)

    def physics(i):
        for g in range(NG):
            receive(2, NG * i + g)
            for h in range(2):
                block = zr[NG * i + g, :, h * 16 : (h + 1) * 16, :].reshape(256, 128).T
                for p in range(4):
                    row = h * 96 + g * 32
                    lhs[row : row + 32, p * 256 : (p + 1) * 256] = block[p * 32 : (p + 1) * 32]

        @pl.loop(0, 4)
        def _(b):
            lanes = pl.ds(pl.multiple_of(b * 256, 256), 256)
            fields[:, lanes] = dot(lhs[...], table[:, lanes])

        row_t = (iota((8, 128), 0) * 0 + ang * NC + i).astype(F32)
        north = (row_t + 0.5) * (math.pi / 384)
        for h in range(2):
            colat = math.pi - north if h == 1 else north
            along = (coriolis * jnp.cos(colat))[0:1, 0:1]
            across = (-coriolis * jnp.sin(colat))[0:1, 0:1]
            weight = (math.pi / 2 * jnp.sin(colat))[0:1, 0:1]

            @pl.loop(0, 4)
            def _(b):
                lanes = pl.ds(pl.multiple_of(b * 256, 256), 256)
                u = [fields[h * 96 + c * 16 : h * 96 + (c + 1) * 16, lanes] for c in range(3)]
                v = [fields[h * 96 + (c + 3) * 16 : h * 96 + (c + 4) * 16, lanes] for c in range(3)]
                w = [flow[c, 2 * i + h, :, lanes].astype(F32) for c in range(3)]
                f = [mag[c, 2 * i + h, :, lanes].astype(F32) for c in range(3)]
                spin = [w[0] + along, w[1] + across, w[2]]
                for c in range(3):
                    n, o = (c + 1) % 3, (c + 2) % 3
                    momentum = (u[n] * spin[o] - u[o] * spin[n]) + (f[n] * v[o] - f[o] * v[n])
                    induction = (u[n] * f[o] - u[o] * f[n]) + (w[n] * v[o] - w[o] * v[n])
                    row = h * 96 + c * 16
                    prods[row : row + 16, lanes] = (momentum * weight).astype(BF16)
                    prods[row + 48 : row + 64, lanes] = (induction * weight).astype(BF16)

        @pl.loop(0, 4)
        def _(p):
            rows = pl.ds(pl.multiple_of(p * 256, 256), 256)
            returned = dot(prods[...], table_back[rows, :], ((1,), (1,)))
            returned = returned.astype(BF16).astype(F32)
            n, s = returned[:96], returned[96:]
            fields[0:96, rows] = n + s
            fields[96:192, rows] = n - s

        for g in range(NG):
            for h in range(2):
                row = h * 96 + g * 32
                block = jnp.concatenate([fields[row : row + 32, p * 256 : (p + 1) * 256] for p in range(4)], axis=0)
                zbs[NG * i + g, :, h * 16 : (h + 1) * 16, :] = block.T.astype(BF16).reshape(NZ, 16, 128)
            send(3, NG * i + g)

    def gather(q):
        receive(3, q)
        ybs[q] = dot(turn[...], zbr[q].reshape(512, 128)).astype(BF16).reshape(NY, 2, 32, 128)
        send(4, q)

    def unfold(q):
        receive(4, q)
        send(5, q)

    def finish(g):
        for i in range(NC):
            receive(5, NG * i + g)
        parts = []
        for b in range(4):
            rows = jnp.concatenate(
                [
                    jnp.concatenate([xbr[NG * i + g, :, 2 * b + e].reshape(128, 128) for i in range(NC)], axis=0)
                    for e in range(2)
                ],
                axis=1,
            )
            first = iota((256, 256), 1) % 128 < 64
            parts.append(jnp.where(first, dot(leg_back[0], rows), dot(leg_back[1], rows)).astype(BF16))
        nonlinear = jnp.concatenate(parts, axis=1)
        for pos in range(2):
            order, top = live_order(pos)
            n = iota((256, 128), 0)
            degree = (order + n).astype(F32)
            damping = jnp.where(n <= top, 1.0 / (1.0 + degree * (degree + 1.0) / 65536.0), 0.0)
            for x in range(2):
                j = pos * 4 + x * 2
                terms = dot(nonlinear, swap[:, j * 128 : (j + 2) * 128]).astype(BF16)
                for cc in range(2):
                    c = 2 * g + cc
                    joined = jnp.concatenate([state[c, x, slot(pos)], terms[:, cc * 128 : (cc + 1) * 128]], axis=1)
                    stepped = dot(joined, ops_ref[c // 3], ((1,), (1,)))
                    out[c, x, slot(pos)] = (stepped * damping).astype(BF16)
        stores[g].start()

    @pl.loop(0, 17)
    def _(step):
        @pl.when(step < 6)
        def _():
            synthesis(step + 3)

        @pl.when(step < NQ)
        def _():
            fold(step)

        @pl.when(jnp.logical_and(step >= 1, step < NQ + 1))
        def _():
            spread(step - 1)

        @pl.when(step == 1)
        def _():
            tables()

        @pl.when(step == 2)
        def _():
            transposed_legendre()
            loads[NG].wait()
            loads[NG + 1].wait()

        for i in range(NC):

            @pl.when(step == 3 * i + 4)
            def _():
                physics(i)

        @pl.when(jnp.logical_and(step >= 7, step < NQ + 7))
        def _():
            gather(step - 7)

        @pl.when(step >= 8)
        def _():
            unfold(step - 8)

        @pl.when(step == 15)
        def _():
            finish(0)

    finish(1)
    finish(2)
    for k in range(6):
        all_sent(k)
    for store in stores:
        store.wait()


def per_device(state, legendre, radial_ops, base_flow, base_field, assign, counts):
    vmem = pl.BlockSpec(memory_space=pltpu.VMEM)
    smem = pl.BlockSpec(memory_space=pltpu.SMEM)
    hbm = pl.BlockSpec(memory_space=pl.ANY)
    dma = pltpu.SemaphoreType.DMA
    assign_rows = assign.T
    return pl.pallas_call(
        kernel,
        out_shape=jax.ShapeDtypeStruct(state.shape, BF16),
        in_specs=[smem, smem, vmem, vmem, vmem, vmem, hbm, hbm, hbm],
        out_specs=hbm,
        scratch_shapes=[
            pltpu.VMEM(state.shape, BF16),
            pltpu.VMEM(base_flow.shape, BF16),
            pltpu.VMEM(base_field.shape, BF16),
            pltpu.VMEM(state.shape, BF16),
            pltpu.VMEM((1024, 1024), BF16),
            pltpu.VMEM((512, 512), BF16),
            pltpu.VMEM((NC, 256, 256), BF16),
            pltpu.VMEM((2, 256, 384), BF16),
            pltpu.VMEM((NG, 256, 1024), BF16),
            pltpu.VMEM((1024, 1024), BF16),
            pltpu.VMEM((1024, 1024), BF16),
            pltpu.VMEM((192, 1024), BF16),
            pltpu.VMEM((192, 1024), F32),
            pltpu.VMEM((192, 1024), BF16),
            pltpu.VMEM((NQ, NX, 32, 1024), BF16),
            pltpu.VMEM((NQ, NX, 32, 1024), BF16),
            pltpu.VMEM((NQ, NY, 2, 32, 128), BF16),
            pltpu.VMEM((NQ, NY, 2, 32, 128), BF16),
            pltpu.VMEM((NQ, NZ, 32, 128), BF16),
            pltpu.VMEM((NQ, NZ, 32, 128), BF16),
            pltpu.VMEM((NQ, NZ, 32, 128), BF16),
            pltpu.VMEM((NQ, NZ, 32, 128), BF16),
            pltpu.VMEM((NQ, NY, 2, 32, 128), BF16),
            pltpu.VMEM((NQ, NY, 2, 32, 128), BF16),
            pltpu.VMEM((NQ, NX, NY, 32, 128), BF16),
            dma((6,)),
            dma((6, NQ)),
            dma((6, NQ)),
            dma((NG + 2,)),
            dma((NG,)),
        ],
        compiler_params=pltpu.CompilerParams(
            collective_id=0, has_side_effects=True, vmem_limit_bytes=56 * 1024 * 1024
        ),
    )(
        assign_rows,
        counts,
        assign_rows,
        counts.reshape(1, -1),
        legendre,
        radial_ops,
        state,
        base_flow,
        base_field,
    )


def solution(mesh):
    placed = (
        P(None, None, ("rad", "ang"), None, None),
        P(("rad", "ang"), None, None),
        P(),
        P(None, "ang", "rad", None),
        P(None, "ang", "rad", None),
        P(),
        P(),
    )
    return jax.shard_map(
        per_device,
        mesh=mesh,
        in_specs=placed,
        out_specs=P(None, None, ("rad", "ang"), None, None),
        check_vma=False,
    )
```

time: 135 us -> 129 us (0.956); the launches traced: 135 us -> 127 us
  Pallas kernels: 128 us -> 125 us
  local copies, waits for them, and re-layouts: 5.1 us -> 2.7 us
  other arithmetic: 1.43 us -> 0 us
    pallas_call x1, Pallas kernels: 128 us -> 125 us  [per_device(): pl.pallas_call(kernel, out_shape=jax.ShapeDtypeStruct(state.shape, BF16),...]
    unnamed x4 -> x1, local copies, waits for them, and re-layouts: 3.93 us -> 2.7 us
where the time goes in v2:
time: 129 us; the launch traced here: 127 us
  Pallas kernels  125 us (97%)
  local copies, waits for them, and re-layouts  2.7 us (2%)
    pallas_call x1, Pallas kernels, per_device(): pl.pallas_call(kernel, out_shape=jax.ShapeDtypeStruct(state.shape, BF16),...  125 us
    unnamed x1, local copies, waits for them, and re-layouts  2.7 us

profile of v2, /device:TPU:1, one launch (start us, length us, event | category | flops | bytes accessed | tf_op | source)
XLA Modules:
  0.0 127.5 jit_solution(18262916312473149532)
XLA Ops:
  0.0 124.8 %shard_map.73 = bf16[6,2,2,256,128]{4,3,2,1,0:T(8,128)(2,1)} custom-call(s32[2,512]{1,0:T(2,128)} %bitcast.2, s32[512]{0:T(512)} %counts_ref.1, s32[2,512]{1,0:T(2,128)} %bitcast.3, s32[1,512]{1,0:T(1,128)} %bitcast.4, bf16[2,192,256]{2,1,0:T(8,128)(2,1)} %leg_ref.1, bf16[2,128,256]{2,1,0:T(8,128)(2,1)} %ops_ref.1, bf16[6,2,2,256,128]{4,3,2,1,0:T(8,128)(2,1)} %state_ref.1, ...), custom_call_target="tpu_custom_call" | custom-call | tf_op jit(solution)/shard_map/pallas_call | solution.py:439
  124.8 2.7 %copy.9 = bf16[6,2,2,256,128]{4,3,2,1,0:T(8,128)(2,1)} copy(bf16[6,2,2,256,128]{4,3,2,1,0:T(8,128)(2,1)} %shard_map.73) | data formatting | bytes 3145728

commit v3 on v2

--- a/solution.py
+++ b/solution.py
@@ -17,6 +17,11 @@
 NC = 3
 NG = 3
 NQ = NC * NG
+AHEAD = 3
+SPREAD_LAG = 2
+PHYSICS_LAG = 7
+GATHER_LAG = 10
+UNFOLD_LAG = 12
 coriolis = 3.0
 
 
@@ -199,7 +204,7 @@
         south = iota((128, 256), 0) // 16 % 2
         return picked, odd_n, south
 
-    for i in range(NC):
+    def forward_legendre(i):
         for pos in range(2):
             picked, odd_n, south = legendre_rows(pos, i)
             leg_fwd[i, pos * 128 : (pos + 1) * 128, :] = jnp.where(odd_n * south == 1, -picked, picked).astype(BF16)
@@ -220,6 +225,7 @@
             xs[q, :, :, b * 256 : (b + 1) * 256] = grid.reshape(NX, 32, 256)
         send(0, q)
 
+    forward_legendre(0)
     shuffle(0)
     pl.semaphore_wait(barrier, NX + NY + NZ - 3)
     synthesis(0)
@@ -227,6 +233,8 @@
     synthesis(1)
     shuffle(2)
     synthesis(2)
+    forward_legendre(1)
+    forward_legendre(2)
 
     a = iota((512, 512), 0)
     b = iota((512, 512), 1)
@@ -380,19 +388,18 @@
                     out[c, x, slot(pos)] = (stepped * damping).astype(BF16)
         stores[g].start()
 
-    @pl.loop(0, 17)
+    def at(step, lag, work, every=1):
+        q = (step - lag) // every
+
+        @pl.when((step >= lag) & (step < lag + NQ) & ((step - lag) % every == 0))
+        def _():
+            work(q)
+
+    @pl.loop(0, UNFOLD_LAG + NQ)
     def _(step):
-        @pl.when(step < 6)
-        def _():
-            synthesis(step + 3)
-
-        @pl.when(step < NQ)
-        def _():
-            fold(step)
-
-        @pl.when(jnp.logical_and(step >= 1, step < NQ + 1))
-        def _():
-            spread(step - 1)
+        at(step, -AHEAD, synthesis)
+        at(step, 0, fold)
+        at(step, SPREAD_LAG, spread)
 
         @pl.when(step == 1)
         def _():
@@ -404,24 +411,11 @@
             loads[NG].wait()
             loads[NG + 1].wait()
 
-        for i in range(NC):
-
-            @pl.when(step == 3 * i + 4)
-            def _():
-                physics(i)
-
-        @pl.when(jnp.logical_and(step >= 7, step < NQ + 7))
-        def _():
-            gather(step - 7)
-
-        @pl.when(step >= 8)
-        def _():
-            unfold(step - 8)
-
-        @pl.when(step == 15)
-        def _():
-            finish(0)
-
+        at(step, PHYSICS_LAG, physics, NG)
+        at(step, GATHER_LAG, gather)
+        at(step, UNFOLD_LAG, unfold)
+
+    finish(0)
     finish(1)
     finish(2)
     for k in range(6):

time: 129 us -> 107 us (0.83)
  Pallas kernels: 125 us -> 104 us
    pallas_call x1, Pallas kernels: 125 us -> 104 us  [per_device(): pl.pallas_call(kernel, out_shape=jax.ShapeDtypeStruct(state.shape, BF16),...]
where the time goes in v3:
time: 107 us; the launch traced here: 106 us
  Pallas kernels  104 us (97%)
  local copies, waits for them, and re-layouts  2.7 us (3%)
    pallas_call x1, Pallas kernels, per_device(): pl.pallas_call(kernel, out_shape=jax.ShapeDtypeStruct(state.shape, BF16),...  104 us
    unnamed x1, local copies, waits for them, and re-layouts  2.7 us

profile of v3, /device:TPU:1, one launch (start us, length us, event | category | flops | bytes accessed | tf_op | source)
XLA Modules:
  0.0 106.5 jit_solution(11792585673130538509)
XLA Ops:
  0.0 103.8 %shard_map.73 = bf16[6,2,2,256,128]{4,3,2,1,0:T(8,128)(2,1)} custom-call(s32[2,512]{1,0:T(2,128)} %bitcast.2, s32[512]{0:T(512)} %counts_ref.1, s32[2,512]{1,0:T(2,128)} %bitcast.3, s32[1,512]{1,0:T(1,128)} %bitcast.4, bf16[2,192,256]{2,1,0:T(8,128)(2,1)} %leg_ref.1, bf16[2,128,256]{2,1,0:T(8,128)(2,1)} %ops_ref.1, bf16[6,2,2,256,128]{4,3,2,1,0:T(8,128)(2,1)} %state_ref.1, ...), custom_call_target="tpu_custom_call" | custom-call | tf_op jit(solution)/shard_map/pallas_call | solution.py:433
  103.8 2.7 %copy.9 = bf16[6,2,2,256,128]{4,3,2,1,0:T(8,128)(2,1)} copy(bf16[6,2,2,256,128]{4,3,2,1,0:T(8,128)(2,1)} %shard_map.73) | data formatting | bytes 3145728

commit v4 on v3

--- a/solution.py
+++ b/solution.py
@@ -17,11 +17,19 @@
 NC = 3
 NG = 3
 NQ = NC * NG
-AHEAD = 3
-SPREAD_LAG = 2
-PHYSICS_LAG = 7
-GATHER_LAG = 10
-UNFOLD_LAG = 12
+SCHEDULE = (
+    ("gather", 12),
+    ("late_table", 7),
+    ("unfold", 14),
+    ("to_grid", 8),
+    ("fold", 0),
+    ("spread", 2),
+    ("products", 8),
+    ("early_table", 0),
+    ("synthesis", -3),
+    ("from_grid", 9),
+    ("transposed_legendre", 4),
+)
 coriolis = 3.0
 
 
@@ -94,7 +102,7 @@
         pltpu.make_async_copy(out.at[2 * g : 2 * g + 2], out_ref.at[2 * g : 2 * g + 2], store_sems.at[g])
         for g in range(NG)
     ]
-    for load in loads:
+    for load in loads[:NG]:
         load.start()
 
     def at_x(x):
@@ -235,6 +243,8 @@
     synthesis(2)
     forward_legendre(1)
     forward_legendre(2)
+    for load in loads[NG:]:
+        load.start()
 
     a = iota((512, 512), 0)
     b = iota((512, 512), 1)
@@ -248,39 +258,39 @@
                 kept = jnp.where(odd_n == south, picked, 0.0)
                 leg_back[pos, :, i * 128 : (i + 1) * 128] = kept.T.astype(BF16)
 
-    def tables():
+    def make_table(pos):
         held = assign_rows_ref[...]
         held = jnp.where(iota((2, 512), 0) < counts_row_ref[...], held, 0)
         digits = jnp.concatenate([held >> 1, held & 1], axis=0).astype(F32).astype(BF16)
-        place = iota((256, 512), 0)
+        place = iota((256, 1), 0)
         place = place // 2 % 8 * 64 + place % 2 * 16 + place // 16
         lane = iota((256, 512), 1)
         low = dot(jnp.where(lane == place, 1.0, 0.0).astype(BF16), digits, ((1,), (1,)))
         high = dot(jnp.where(lane == place + 32, 1.0, 0.0).astype(BF16), digits, ((1,), (1,)))
+        m = 2.0 * (low[:, pos : pos + 1] + high[:, 1 - pos : 2 - pos]) + (
+            low[:, 2 + pos : 3 + pos] + high[:, 3 - pos : 4 - pos]
+        )
+        m = m.astype(jnp.int32)
+        fine = (m * iota((256, 128), 1) & 1023).astype(F32) * (2.0 * math.pi / 1024)
         scale = 1.0 / math.sqrt(512)
-        for pos in range(2):
-            m = 2.0 * (low[:, pos : pos + 1] + high[:, 1 - pos : 2 - pos]) + (
-                low[:, 2 + pos : 3 + pos] + high[:, 3 - pos : 4 - pos]
-            )
-            m = m.astype(jnp.int32)
-            lane = iota((256, 128), 1)
-            fine = (m * lane & 1023).astype(F32) * (2.0 * math.pi / 1024)
-            cos_fine = jnp.cos(fine) * scale
-            sin_fine = jnp.sin(fine) * scale
-            coarse = (m * lane & 7).astype(F32) * (2.0 * math.pi / 8)
-            cos_coarse = jnp.cos(coarse)
-            sin_coarse = jnp.sin(coarse)
-            back = jnp.where(m == 0, 0.5, 1.0)
-            for k in range(8):
-                ck = cos_coarse[:, k : k + 1]
-                sk = sin_coarse[:, k : k + 1]
-                re = (cos_fine * ck - sin_fine * sk).astype(BF16)
-                im = (-(sin_fine * ck + cos_fine * sk)).astype(BF16)
-                lanes = slice(k * 128, (k + 1) * 128)
-                table[pos * 512 : pos * 512 + 256, lanes] = re
-                table[pos * 512 + 256 : pos * 512 + 512, lanes] = im
-                table_back[pos * 512 : pos * 512 + 256, lanes] = (re.astype(F32) * back).astype(BF16)
-                table_back[pos * 512 + 256 : pos * 512 + 512, lanes] = (im.astype(F32) * back).astype(BF16)
+        cos_at = jnp.cos(fine)
+        sin_at = jnp.sin(fine)
+        half_cos = cos_at[:, 64:65]
+        half_sin = sin_at[:, 64:65]
+        cos_step = 1.0 - 2.0 * half_sin * half_sin
+        sin_step = 2.0 * half_sin * half_cos
+        cos_at = cos_at * scale
+        sin_at = sin_at * scale
+        back = jnp.where(m == 0, 0.5, 1.0)
+        for k in range(8):
+            re = cos_at.astype(BF16)
+            im = (-sin_at).astype(BF16)
+            lanes = slice(k * 128, (k + 1) * 128)
+            table[pos * 512 : pos * 512 + 256, lanes] = re
+            table[pos * 512 + 256 : pos * 512 + 512, lanes] = im
+            table_back[pos * 512 : pos * 512 + 256, lanes] = (re.astype(F32) * back).astype(BF16)
+            table_back[pos * 512 + 256 : pos * 512 + 512, lanes] = (im.astype(F32) * back).astype(BF16)
+            cos_at, sin_at = cos_at * cos_step - sin_at * sin_step, sin_at * cos_step + cos_at * sin_step
 
     def fold(q):
         receive(0, q)
@@ -295,7 +305,7 @@
         zs[q] = dot(turn[...], yr[q].reshape(512, 128)).astype(BF16).reshape(NZ, 32, 128)
         send(2, q)
 
-    def physics(i):
+    def to_grid(i):
         for g in range(NG):
             receive(2, NG * i + g)
             for h in range(2):
@@ -309,6 +319,7 @@
             lanes = pl.ds(pl.multiple_of(b * 256, 256), 256)
             fields[:, lanes] = dot(lhs[...], table[:, lanes])
 
+    def products(i):
         row_t = (iota((8, 128), 0) * 0 + ang * NC + i).astype(F32)
         north = (row_t + 0.5) * (math.pi / 384)
         for h in range(2):
@@ -333,6 +344,7 @@
                     prods[row : row + 16, lanes] = (momentum * weight).astype(BF16)
                     prods[row + 48 : row + 64, lanes] = (induction * weight).astype(BF16)
 
+    def from_grid(i):
         @pl.loop(0, 4)
         def _(p):
             rows = pl.ds(pl.multiple_of(p * 256, 256), 256)
@@ -388,32 +400,38 @@
                     out[c, x, slot(pos)] = (stepped * damping).astype(BF16)
         stores[g].start()
 
-    def at(step, lag, work, every=1):
-        q = (step - lag) // every
-
-        @pl.when((step >= lag) & (step < lag + NQ) & ((step - lag) % every == 0))
-        def _():
-            work(q)
-
-    @pl.loop(0, UNFOLD_LAG + NQ)
+    by_piece = {"synthesis": synthesis, "fold": fold, "spread": spread, "gather": gather, "unfold": unfold}
+    by_chunk = {"to_grid": to_grid, "products": products, "from_grid": from_grid}
+
+    def late_table():
+        make_table(1)
+        loads[NG].wait()
+        loads[NG + 1].wait()
+
+    once = {
+        "early_table": lambda: make_table(0),
+        "late_table": late_table,
+        "transposed_legendre": transposed_legendre,
+    }
+
+    @pl.loop(0, max(lag for _, lag in SCHEDULE) + NQ)
     def _(step):
-        at(step, -AHEAD, synthesis)
-        at(step, 0, fold)
-        at(step, SPREAD_LAG, spread)
-
-        @pl.when(step == 1)
-        def _():
-            tables()
-
-        @pl.when(step == 2)
-        def _():
-            transposed_legendre()
-            loads[NG].wait()
-            loads[NG + 1].wait()
-
-        at(step, PHYSICS_LAG, physics, NG)
-        at(step, GATHER_LAG, gather)
-        at(step, UNFOLD_LAG, unfold)
+        for what, lag in SCHEDULE:
+            if what in once:
+                due = step == lag
+            else:
+                due = (step >= lag) & (step < lag + NQ)
+            if what in by_chunk:
+                due &= (step - lag) % NG == 0
+
+            @pl.when(due)
+            def _():
+                if what in once:
+                    once[what]()
+                elif what in by_chunk:
+                    by_chunk[what]((step - lag) // NG)
+                else:
+                    by_piece[what](step - lag)
 
     finish(0)
     finish(1)

time: 107 us -> 105 us (0.981)
  Pallas kernels: 104 us -> 102 us
    pallas_call x1, Pallas kernels: 104 us -> 102 us  [per_device(): pl.pallas_call(kernel, out_shape=jax.ShapeDtypeStruct(state.shape, BF16),...]
where the time goes in v4:
time: 105 us
  Pallas kernels  102 us (97%)
  local copies, waits for them, and re-layouts  2.7 us (3%)
    pallas_call x1, Pallas kernels, per_device(): pl.pallas_call(kernel, out_shape=jax.ShapeDtypeStruct(state.shape, BF16),...  102 us
    unnamed x1, local copies, waits for them, and re-layouts  2.7 us

profile of v4, /device:TPU:1, one launch (start us, length us, event | category | flops | bytes accessed | tf_op | source)
XLA Modules:
  0.0 105.2 jit_solution(3115313480089758656)
XLA Ops:
  0.0 102.4 %shard_map.73 = bf16[6,2,2,256,128]{4,3,2,1,0:T(8,128)(2,1)} custom-call(s32[2,512]{1,0:T(2,128)} %bitcast.2, s32[512]{0:T(512)} %counts_ref.1, s32[2,512]{1,0:T(2,128)} %bitcast.3, s32[1,512]{1,0:T(1,128)} %bitcast.4, bf16[2,192,256]{2,1,0:T(8,128)(2,1)} %leg_ref.1, bf16[2,128,256]{2,1,0:T(8,128)(2,1)} %ops_ref.1, bf16[6,2,2,256,128]{4,3,2,1,0:T(8,128)(2,1)} %state_ref.1, ...), custom_call_target="tpu_custom_call" | custom-call | tf_op jit(solution)/shard_map/pallas_call | solution.py:451
  102.5 2.7 %copy.9 = bf16[6,2,2,256,128]{4,3,2,1,0:T(8,128)(2,1)} copy(bf16[6,2,2,256,128]{4,3,2,1,0:T(8,128)(2,1)} %shard_map.73) | data formatting | bytes 3145728

commit v5 on v4

--- a/solution.py
+++ b/solution.py
@@ -16,19 +16,24 @@
 NY = 8
 NC = 3
 NG = 3
-NQ = NC * NG
+NP = NC * NG
+NQ = 2 * NP
 SCHEDULE = (
-    ("gather", 12),
-    ("late_table", 7),
-    ("unfold", 14),
-    ("to_grid", 8),
-    ("fold", 0),
-    ("spread", 2),
-    ("products", 8),
-    ("early_table", 0),
-    ("synthesis", -3),
-    ("from_grid", 9),
-    ("transposed_legendre", 4),
+    ("to_grid", 0, 8),
+    ("early_table", 0, 1),
+    ("transposed_legendre", 0, 3),
+    ("unfold", 0, 14),
+    ("fold", 1, 1),
+    ("middle", 1, 3),
+    ("products", 0, 8),
+    ("unfold", 1, 14),
+    ("gather", 1, 11),
+    ("late_table", 0, 6),
+    ("gather", 0, 11),
+    ("synthesis", 0, -3),
+    ("from_grid", 0, 9),
+    ("middle", 0, 2),
+    ("fold", 0, 0),
 )
 coriolis = 3.0
 
@@ -206,16 +211,19 @@
         rows = leg_ref[slot(pos)]
         rows = jnp.where(iota((192, 256), 1) <= top, rows.astype(F32), 0.0).astype(BF16)
         r = iota((128, 192), 0)
-        pick = jnp.where(iota((128, 192), 1) == 3 * (r // 32 * 16 + r % 16) + i, 1.0, 0.0).astype(BF16)
+        pick = jnp.where(iota((128, 192), 1) == 3 * (r % 64) + i, 1.0, 0.0).astype(BF16)
         picked = dot(pick, rows)
         odd_n = iota((128, 256), 1) % 2
-        south = iota((128, 256), 0) // 16 % 2
+        south = iota((128, 256), 0) // 64
         return picked, odd_n, south
 
     def forward_legendre(i):
         for pos in range(2):
             picked, odd_n, south = legendre_rows(pos, i)
-            leg_fwd[i, pos * 128 : (pos + 1) * 128, :] = jnp.where(odd_n * south == 1, -picked, picked).astype(BF16)
+            signed = jnp.where(odd_n * south == 1, -picked, picked).astype(BF16)
+            for h in range(2):
+                row = h * 128 + pos * 64
+                leg_fwd[i, row : row + 64, :] = signed[h * 64 : (h + 1) * 64]
 
     def shuffle(g):
         loads[g].wait()
@@ -225,13 +233,16 @@
         for b in range(4):
             coeffs[g, :, b * 256 : (b + 1) * 256] = dot(joined, swap[:, b * 256 : (b + 1) * 256]).astype(BF16)
 
-    def synthesis(q):
-        first = iota((128, 256), 1) % 128 < 64
+    def synthesis(j):
+        first = iota((64, 256), 1) % 128 < 64
         for b in range(4):
-            both = dot(leg_fwd[q // NG], coeffs[q % NG, :, b * 256 : (b + 1) * 256])
-            grid = jnp.where(first, both[:128], both[128:]).astype(BF16)
-            xs[q, :, :, b * 256 : (b + 1) * 256] = grid.reshape(NX, 32, 256)
-        send(0, q)
+            both = dot(leg_fwd[j // NG], coeffs[j % NG, :, b * 256 : (b + 1) * 256])
+            for h in range(2):
+                row = h * 128
+                grid = jnp.where(first, both[row : row + 64], both[row + 64 : row + 128]).astype(BF16)
+                xs[2 * j + h, :, :, b * 256 : (b + 1) * 256] = grid.reshape(NX, 16, 256)
+        send(0, 2 * j)
+        send(0, 2 * j + 1)
 
     forward_legendre(0)
     shuffle(0)
@@ -246,10 +257,18 @@
     for load in loads[NG:]:
         load.start()
 
-    a = iota((512, 512), 0)
-    b = iota((512, 512), 1)
-    image = (a % 16) * 32 + a // 16 % 2 * 16 + a // 32
-    turn[...] = jnp.where(b == image, 1.0, 0.0).astype(BF16)
+    a = iota((256, 256), 0)
+    b = iota((256, 256), 1)
+    turn[...] = jnp.where(b == a % 16 * 16 + a // 16, 1.0, 0.0).astype(BF16)
+
+    def turned(rows):
+        return dot(turn[...], rows.reshape(256, 128)).astype(BF16)
+
+    def by_y(rows):
+        return rows.reshape(NY, 2, 16, 128)
+
+    def by_z(rows):
+        return rows.reshape(NZ, 16, 128)
 
     def transposed_legendre():
         for i in range(NC):
@@ -292,24 +311,41 @@
             table_back[pos * 512 + 256 : pos * 512 + 512, lanes] = (im.astype(F32) * back).astype(BF16)
             cos_at, sin_at = cos_at * cos_step - sin_at * sin_step, sin_at * cos_step + cos_at * sin_step
 
-    def fold(q):
+    def fold(j, h):
+        q = 2 * j + h
         receive(0, q)
-        for p in range(2):
-            pair = xr[q, p] + xr[q, p + 2]
+        pairs = [xr[q, p] + xr[q, p + 2] for p in range(2)]
+        if h == 0:
             for y in range(NY):
-                ys[q, y, p] = pair[:, y * 128 : (y + 1) * 128]
-        send(1, q)
-
-    def spread(q):
-        receive(1, q)
-        zs[q] = dot(turn[...], yr[q].reshape(512, 128)).astype(BF16).reshape(NZ, 32, 128)
-        send(2, q)
+                for p in range(2):
+                    ys[q, y, p] = pairs[p][:, y * 128 : (y + 1) * 128]
+            send(1, q)
+        else:
+            rows = [pairs[p][:, y * 128 : (y + 1) * 128] for y in range(NY) for p in range(2)]
+            zs[q] = by_z(turned(jnp.concatenate(rows, axis=0)))
+            send(2, q)
+
+    def middle(j, h):
+        q = 2 * j + h
+        if h == 0:
+            receive(1, q)
+            zs[q] = by_z(turned(yr[q]))
+            send(2, q)
+        else:
+            receive(2, q)
+            ys[q] = by_y(turned(zr[q]))
+            send(1, q)
 
     def to_grid(i):
         for g in range(NG):
-            receive(2, NG * i + g)
             for h in range(2):
-                block = zr[NG * i + g, :, h * 16 : (h + 1) * 16, :].reshape(256, 128).T
+                q = 2 * (NG * i + g) + h
+                if h == 0:
+                    receive(2, q)
+                    block = zr[q].reshape(256, 128).T
+                else:
+                    receive(1, q)
+                    block = turned(yr[q]).T
                 for p in range(4):
                     row = h * 96 + g * 32
                     lhs[row : row + 32, p * 256 : (p + 1) * 256] = block[p * 32 : (p + 1) * 32]
@@ -358,26 +394,44 @@
             for h in range(2):
                 row = h * 96 + g * 32
                 block = jnp.concatenate([fields[row : row + 32, p * 256 : (p + 1) * 256] for p in range(4)], axis=0)
-                zbs[NG * i + g, :, h * 16 : (h + 1) * 16, :] = block.T.astype(BF16).reshape(NZ, 16, 128)
-            send(3, NG * i + g)
-
-    def gather(q):
-        receive(3, q)
-        ybs[q] = dot(turn[...], zbr[q].reshape(512, 128)).astype(BF16).reshape(NY, 2, 32, 128)
-        send(4, q)
-
-    def unfold(q):
-        receive(4, q)
+                block = block.T.astype(BF16)
+                q = 2 * (NG * i + g) + h
+                if h == 0:
+                    zbs[q] = by_z(block)
+                    send(3, q)
+                else:
+                    ybs[q] = by_y(turned(block))
+                    send(4, q)
+
+    def gather(j, h):
+        q = 2 * j + h
+        if h == 0:
+            receive(3, q)
+            ybs[q] = by_y(turned(zbr[q]))
+            send(4, q)
+        else:
+            receive(4, q)
+            zbs[q] = by_z(turned(ybr[q]))
+            send(3, q)
+
+    def unfold(j, h):
+        q = 2 * j + h
+        if h == 0:
+            receive(4, q)
+        else:
+            receive(3, q)
+            ybr[q] = by_y(turned(zbr[q]))
         send(5, q)
 
     def finish(g):
-        for i in range(NC):
-            receive(5, NG * i + g)
+        pieces = [2 * (NG * i + g) + h for i in range(NC) for h in range(2)]
+        for q in pieces:
+            receive(5, q)
         parts = []
         for b in range(4):
             rows = jnp.concatenate(
                 [
-                    jnp.concatenate([xbr[NG * i + g, :, 2 * b + e].reshape(128, 128) for i in range(NC)], axis=0)
+                    jnp.concatenate([xbr[q, :, 2 * b + e].reshape(64, 128) for q in pieces], axis=0)
                     for e in range(2)
                 ],
                 axis=1,
@@ -400,7 +454,7 @@
                     out[c, x, slot(pos)] = (stepped * damping).astype(BF16)
         stores[g].start()
 
-    by_piece = {"synthesis": synthesis, "fold": fold, "spread": spread, "gather": gather, "unfold": unfold}
+    by_piece = {"fold": fold, "middle": middle, "gather": gather, "unfold": unfold}
     by_chunk = {"to_grid": to_grid, "products": products, "from_grid": from_grid}
 
     def late_table():
@@ -414,13 +468,13 @@
         "transposed_legendre": transposed_legendre,
     }
 
-    @pl.loop(0, max(lag for _, lag in SCHEDULE) + NQ)
+    @pl.loop(0, max(lag for _, _, lag in SCHEDULE) + NP)
     def _(step):
-        for what, lag in SCHEDULE:
+        for what, h, lag in SCHEDULE:
             if what in once:
                 due = step == lag
             else:
-                due = (step >= lag) & (step < lag + NQ)
+                due = (step >= lag) & (step < lag + NP)
             if what in by_chunk:
                 due &= (step - lag) % NG == 0
 
@@ -430,8 +484,10 @@
                     once[what]()
                 elif what in by_chunk:
                     by_chunk[what]((step - lag) // NG)
+                elif what == "synthesis":
+                    synthesis(step - lag)
                 else:
-                    by_piece[what](step - lag)
+                    by_piece[what](step - lag, h)
 
     finish(0)
     finish(1)
@@ -459,7 +515,7 @@
             pltpu.VMEM(base_field.shape, BF16),
             pltpu.VMEM(state.shape, BF16),
             pltpu.VMEM((1024, 1024), BF16),
-            pltpu.VMEM((512, 512), BF16),
+            pltpu.VMEM((256, 256), BF16),
             pltpu.VMEM((NC, 256, 256), BF16),
             pltpu.VMEM((2, 256, 384), BF16),
             pltpu.VMEM((NG, 256, 1024), BF16),
@@ -468,17 +524,17 @@
             pltpu.VMEM((192, 1024), BF16),
             pltpu.VMEM((192, 1024), F32),
             pltpu.VMEM((192, 1024), BF16),
-            pltpu.VMEM((NQ, NX, 32, 1024), BF16),
-            pltpu.VMEM((NQ, NX, 32, 1024), BF16),
-            pltpu.VMEM((NQ, NY, 2, 32, 128), BF16),
-            pltpu.VMEM((NQ, NY, 2, 32, 128), BF16),
-            pltpu.VMEM((NQ, NZ, 32, 128), BF16),
-            pltpu.VMEM((NQ, NZ, 32, 128), BF16),
-            pltpu.VMEM((NQ, NZ, 32, 128), BF16),
-            pltpu.VMEM((NQ, NZ, 32, 128), BF16),
-            pltpu.VMEM((NQ, NY, 2, 32, 128), BF16),
-            pltpu.VMEM((NQ, NY, 2, 32, 128), BF16),
-            pltpu.VMEM((NQ, NX, NY, 32, 128), BF16),
+            pltpu.VMEM((NQ, NX, 16, 1024), BF16),
+            pltpu.VMEM((NQ, NX, 16, 1024), BF16),
+            pltpu.VMEM((NQ, NY, 2, 16, 128), BF16),
+            pltpu.VMEM((NQ, NY, 2, 16, 128), BF16),
+            pltpu.VMEM((NQ, NZ, 16, 128), BF16),
+            pltpu.VMEM((NQ, NZ, 16, 128), BF16),
+            pltpu.VMEM((NQ, NZ, 16, 128), BF16),
+            pltpu.VMEM((NQ, NZ, 16, 128), BF16),
+            pltpu.VMEM((NQ, NY, 2, 16, 128), BF16),
+            pltpu.VMEM((NQ, NY, 2, 16, 128), BF16),
+            pltpu.VMEM((NQ, NX, NY, 16, 128), BF16),
             dma((6,)),
             dma((6, NQ)),
             dma((6, NQ)),

time: 105 us -> 99.8 us (0.950); the launches traced: 105 us -> 98.7 us
  Pallas kernels: 102 us -> 96 us
    pallas_call x1, Pallas kernels: 102 us -> 96 us  [per_device(): pl.pallas_call(kernel, out_shape=jax.ShapeDtypeStruct(state.shape, BF16),...]
where the time goes in v5:
time: 99.8 us; the launch traced here: 98.7 us
  Pallas kernels  96 us (96%)
  local copies, waits for them, and re-layouts  2.7 us (3%)
    pallas_call x1, Pallas kernels, per_device(): pl.pallas_call(kernel, out_shape=jax.ShapeDtypeStruct(state.shape, BF16),...  96 us
    unnamed x1, local copies, waits for them, and re-layouts  2.7 us

profile of v5, /device:TPU:1, one launch (start us, length us, event | category | flops | bytes accessed | tf_op | source)
XLA Modules:
  0.0 98.7 jit_solution(12835798116539021071)
XLA Ops:
  0.0 96.0 %shard_map.73 = bf16[6,2,2,256,128]{4,3,2,1,0:T(8,128)(2,1)} custom-call(s32[2,512]{1,0:T(2,128)} %bitcast.2, s32[512]{0:T(512)} %counts_ref.1, s32[2,512]{1,0:T(2,128)} %bitcast.3, s32[1,512]{1,0:T(1,128)} %bitcast.4, bf16[2,192,256]{2,1,0:T(8,128)(2,1)} %leg_ref.1, bf16[2,128,256]{2,1,0:T(8,128)(2,1)} %ops_ref.1, bf16[6,2,2,256,128]{4,3,2,1,0:T(8,128)(2,1)} %state_ref.1, ...), custom_call_target="tpu_custom_call" | custom-call | tf_op jit(solution)/shard_map/pallas_call | solution.py:507
  96.0 2.7 %copy.9 = bf16[6,2,2,256,128]{4,3,2,1,0:T(8,128)(2,1)} copy(bf16[6,2,2,256,128]{4,3,2,1,0:T(8,128)(2,1)} %shard_map.73) | data formatting | bytes 3145728
